TPU v7x, 32 devices: a whole 2x2x4 slice. The times are simulated.
32 devices in a mesh: freq: 16 (over z, y, x), panel: 2 (over core).
Axes of the slice: x: 2, y: 2, z: 4, core: 2. Of those that a mesh axis runs over, the one named last changes fastest.
Arguments:
- shot_gathers: bfloat16 [64, 2048, 2048], P('freq', 'panel'), may hold values from -6 to 6
- aperture_blocks: int32 [32], replicated, may hold values from 8 to 16, as said below
- taper_index: int32 [32], replicated, may hold values from 0 to 3
Outputs:
- predicted: bfloat16 [64, 2048, 128], P('freq', 'panel')
Inputs may be any that keep to these rules, and one draw needn't show every extreme that they name: `aperture_blocks`: aperture of each frequency in blocks of 128 surface points, counted from the first point; the largest value occurs in every draw.
All inputs are finite; a program needn't handle non-finite values.
Results may differ from a plain program's by a relative error of at most 0.0076.
Values may be sent and summed in bfloat16 or wider, within the bound.
A program may use at most 128 MiB of HBM per device.

v0:
```python
import math

import jax
import jax.numpy as jnp
from jax import lax
from jax.sharding import PartitionSpec as P

SW = 128
BLOCK = 128
F_DEV = 2
TAPER = 64


def transform_tables(freq_total, time_total):
    bins = jnp.arange(freq_total, dtype=jnp.int32) + 1
    times = jnp.arange(time_total, dtype=jnp.int32)
    phase = bins[:, None] * times[None, :] % time_total
    angle = phase.astype(jnp.float32) * (2.0 * math.pi / time_total)
    scale = 1.0 / math.sqrt(time_total)
    forward = jnp.stack([jnp.cos(angle) * scale, -jnp.sin(angle) * scale], axis=1).astype(
        jnp.bfloat16
    )
    inverse = jnp.stack([jnp.cos(angle), -jnp.sin(angle)], axis=1).astype(jnp.bfloat16)
    return (forward, inverse)


def taper_weights(aperture, taper_level, surface_points):
    ends = aperture * BLOCK
    ramp = jnp.minimum(TAPER * (1 + taper_level), ends)
    begins = ends - ramp
    offset = (surface_points - begins + 1).astype(jnp.float32)
    wave = jnp.cos(0.5 * math.pi * offset / (ramp + 1).astype(jnp.float32))
    inside = jnp.where(surface_points < ends, wave * wave, jnp.zeros_like(wave))
    return jnp.where(surface_points < begins, jnp.ones_like(wave), inside)


def body(shot_gathers, aperture_blocks, taper_index):
    time_local, rows_local, points_total = shot_gathers.shape
    owners = lax.axis_size("freq")
    slot_count = 2 * F_DEV
    time_total = time_local * owners
    freq_total = F_DEV * owners
    owner_index = lax.axis_index("freq")
    panel_index = lax.axis_index("panel")
    owner_range = jnp.arange(owners, dtype=jnp.int32)
    freq_range = jnp.arange(freq_total, dtype=jnp.int32)
    assignment = freq_range.reshape(owners, F_DEV)
    forward, inverse = transform_tables(freq_total, time_total)
    selector = (assignment.reshape(-1)[:, None] == freq_range[None, :]).astype(jnp.bfloat16)
    picked_forward = jnp.dot(
        selector, forward.reshape(freq_total, 2 * time_total), preferred_element_type=jnp.float32
    ).astype(jnp.bfloat16)
    forward_rows = (
        picked_forward.reshape(owners, F_DEV, 2, time_total)
        .transpose(1, 2, 0, 3)
        .reshape(slot_count, owners, time_total)
    )
    picked_inverse = jnp.dot(
        selector, inverse.reshape(freq_total, 2 * time_total), preferred_element_type=jnp.float32
    ).astype(jnp.bfloat16)
    inverse_rows = picked_inverse.reshape(owners * slot_count, owners, time_local)
    trace_width = rows_local * points_total // owners
    outgoing_time = shot_gathers.reshape(time_local, owners, trace_width)
    series = lax.all_to_all(outgoing_time, "freq", split_axis=1, concat_axis=0, tiled=True)[:, 0, :]
    spectra = jnp.einsum(
        "qot,tw->qow", forward_rows, series, preferred_element_type=jnp.float32
    ).astype(jnp.bfloat16)
    own_spectra = lax.all_to_all(spectra, "freq", split_axis=1, concat_axis=1, tiled=True)
    own_spectra = own_spectra.reshape(F_DEV, 2, rows_local, points_total)
    mine = owner_range[:, None] == owner_index
    my_freqs = jnp.sum(jnp.where(mine, assignment, jnp.zeros_like(assignment)), axis=0)
    matches = my_freqs[:, None] == freq_range[None, :]
    my_aperture = jnp.sum(jnp.where(matches, aperture_blocks[None, :], 0), axis=1)
    my_taper = jnp.sum(jnp.where(matches, taper_index[None, :], 0), axis=1)
    local_points = panel_index * rows_local + jnp.arange(rows_local, dtype=jnp.int32)
    weights = taper_weights(my_aperture[:, None], my_taper[:, None], local_points[None, :])
    tapered = (weights[:, None, :, None] * own_spectra[:, :, :, :SW].astype(jnp.float32)).astype(
        jnp.bfloat16
    )
    piece = lax.all_gather(tapered, "panel", axis=2, tiled=True)
    updated_list = []
    for slot_index in range(F_DEV):
        left_block = own_spectra[slot_index]
        stacked_left = jnp.concatenate([left_block[0], left_block[1]], axis=1)
        real_side = jnp.concatenate([piece[slot_index, 0], -piece[slot_index, 1]], axis=0)
        imag_side = jnp.concatenate([piece[slot_index, 1], piece[slot_index, 0]], axis=0)
        stacked_right = jnp.stack([real_side, imag_side], axis=0)
        updated = jnp.einsum(
            "rk,cks->crs", stacked_left, stacked_right, preferred_element_type=jnp.float32
        )
        updated_list.append(updated)
    summed = jnp.stack(updated_list, axis=0)
    multiples = (summed * (-1.0 / math.sqrt(points_total))).astype(jnp.bfloat16)
    output_width = rows_local * SW // owners
    outgoing_freq = multiples.reshape(slot_count, owners, output_width)
    output_scale = 1.0 / math.sqrt(freq_total)
    values = lax.all_to_all(outgoing_freq, "freq", split_axis=1, concat_axis=0, tiled=True)[:, 0, :]
    traces = (
        jnp.einsum("qgt,qw->tgw", inverse_rows, values, preferred_element_type=jnp.float32)
        * output_scale
    )
    result = lax.all_to_all(
        traces.astype(jnp.bfloat16), "freq", split_axis=1, concat_axis=1, tiled=True
    )
    return result.reshape(time_local, rows_local, SW)


def solution(mesh):
    return jax.shard_map(
        body,
        mesh=mesh,
        in_specs=(P("freq", "panel", None), P(), P()),
        out_specs=P("freq", "panel", None),
        check_vma=False,
    )
```

profile of v0, /device:TPU:0, one launch (start us, length us, event | category | flops | bytes accessed | tf_op | source)
XLA Modules:
  0.0 1098.2 jit_solution(10738489167989122141)
XLA Ops:
  6.5 17.0 %reshape.339 = bf16[4,16,131072]{2,1,0:T(8,128)(2,1)} reshape(bf16[4,1024,2048]{2,1,0:T(8,128)(2,1)} %param.3) | data formatting | bytes 33554432 | tf_op jit(solution)/shard_map/reshape | solution.py:63
  23.5 22.1 %copy.53 = bf16[4,16,131072]{2,0,1:T(4,128)(2,1)} copy(bf16[4,16,131072]{2,1,0:T(8,128)(2,1)} %reshape.339) | data formatting | bytes 33554432 | tf_op jit(solution)/shard_map/reshape | solution.py:63
  45.6 8.4 all-to-all-start
  54.0 0.2 fusion.29
  54.2 0.1 convert_element_type.85
  54.3 0.1 convolution_convert_fusion.2
  54.4 0.1 reshape.337
  54.5 314.8 %all-to-all-done = bf16[4,16,131072]{2,0,1:T(4,128)(2,1)} async-done(((bf16[4,16,131072]{2,0,1:T(4,128)(2,1)}), bf16[4,16,131072]{2,0,1:T(4,128)(2,1)}, u32[]{:S(2)}, u32[]{:S(2)}) %all-to-all-start) | async-done | bytes 16777248 | tf_op jit(solution)/shard_map/all_to_all | solution.py:64
  369.3 15.0 %reshape.343 = bf16[64,131072,1]{1,0,2:T(8,128)(2,1)} reshape(bf16[16,4,1,131072]{3,1,0,2:T(4,128)(2,1)} %bitcast.3) | data formatting | bytes 33554432 | tf_op jit(solution)/shard_map/squeeze | solution.py:64
  384.4 11.4 %convolution_convert_fusion = bf16[4,16,131072]{2,1,0:T(8,128)(2,1)} fusion(bf16[4,16,64]{2,1,0:T(8,128)(2,1)S(1)} %bitcast.61, bf16[64,131072,1]{1,0,2:T(8,128)(2,1)} %reshape.343), kind=kOutput, calls=%fused_computation | convolution fusion | flops 1082130432 | bytes 33562624 | tf_op jit(solution)/shard_map/qot,tw->qow/dot_general | solution.py:65
  395.8 22.1 %copy.54 = bf16[4,16,131072]{2,0,1:T(4,128)(2,1)} copy(bf16[4,16,131072]{2,1,0:T(8,128)(2,1)} %convolution_convert_fusion) | data formatting | bytes 33554432 | tf_op jit(solution)/shard_map/convert_element_type | solution.py:67
  417.9 0.0 copy-start.4
  417.9 0.0 copy-start.5
  417.9 73.2 %all-to-all-start.1 = ((bf16[4,16,131072]{2,0,1:T(4,128)(2,1)}), bf16[4,16,131072]{2,0,1:T(4,128)(2,1)}, u32[]{:S(2)}, u32[]{:S(2)}) async-start(bf16[4,16,131072]{2,0,1:T(4,128)(2,1)} %copy.54), calls=%async_computation.1 | async-start | bytes 33554432 | tf_op jit(solution)/shard_map/all_to_all | solution.py:68
  491.1 0.2 all-gather.2.cloned.1.call-start
  491.4 0.1 select_reduce_fusion.2
  491.5 0.0 copy-done.4
  491.5 0.0 copy-done.5
  491.5 0.2 select_reduce_fusion.1
  491.7 0.2 compare_select_fusion.1
  491.9 311.9 %all-to-all-done.1 = bf16[4,16,131072]{2,0,1:T(4,128)(2,1)} async-done(((bf16[4,16,131072]{2,0,1:T(4,128)(2,1)}), bf16[4,16,131072]{2,0,1:T(4,128)(2,1)}, u32[]{:S(2)}, u32[]{:S(2)}) %all-to-all-start.1) | async-done | bytes 16777248 | tf_op jit(solution)/shard_map/all_to_all | solution.py:68
  803.8 18.5 %copy.55 = bf16[4,16,131072]{2,1,0:T(8,128)(2,1)} copy(bf16[4,16,131072]{2,0,1:T(4,128)(2,1)} %all-to-all-done.1) | data formatting | bytes 33554432 | tf_op jit(solution)/shard_map/all_to_all | solution.py:68
  822.3 17.0 %reshape.340 = bf16[2,2,1024,2048]{3,2,1,0:T(8,128)(2,1)} reshape(bf16[4,16,131072]{2,1,0:T(8,128)(2,1)} %copy.55) | data formatting | bytes 33554432 | tf_op jit(solution)/shard_map/reshape | solution.py:69
  839.3 1.3 slice.52
  840.6 0.5 copy.63
  841.2 1.2 multiply_convert_fusion
  842.4 0.0 all-gather.2.cloned.1.call-update
  842.4 86.1 %slice_reduce_fusion.3 = (bf16[16,131072]{1,0:T(8,128)(2,1)}, bf16[16,131072]{1,0:T(8,128)(2,1)}, bf16[16,131072]{1,0:T(8,128)(2,1)}, bf16[16,131072]{1,0:T(8,128)(2,1)}) fusion(bf16[4,16,131072]{2,0,1:T(4,128)(2,1)} %all-to-all-done.1), kind=kLoop, calls=%fused_computation.7 | loop fusion | bytes 33554432 | tf_op jit(solution)/shard_map/slice | solution.py:84
  928.5 4.8 squeeze.44
  933.3 4.8 squeeze.43
  938.1 4.8 squeeze.40
  942.9 4.8 squeeze.39
  947.8 0.0 all-gather.2.cloned.1.call-done
  947.8 1.3 fusion.33
  949.0 0.0 copy-start.3
  949.0 1.8 slice_bitcast_fusion.2
  950.8 0.0 copy-start.1
  950.9 0.2 maximum_bitcast_fusion.10
  951.1 0.2 maximum_bitcast_fusion.8
  951.3 0.5 copy-done.3
  951.8 1.5 copy-done.1
  953.4 0.0 copy-start
  953.4 0.0 copy-start.2
  953.4 2.4 fusion.15
  955.7 0.0 copy-done
  955.7 1.1 copy-done.2
  956.8 2.4 fusion.18
  959.2 0.3 fusion.14
  959.5 0.7 copy.57
  960.1 0.8 convert_element_type.91
  960.9 1.8 copy.58
  962.7 72.7 %all-to-all-start.2 = ((bf16[4,16,8192]{2,0,1:T(4,128)(2,1)}), bf16[4,16,8192]{2,0,1:T(4,128)(2,1)S(1)}, u32[]{:S(2)}, u32[]{:S(2)}) async-start(bf16[4,16,8192]{2,0,1:T(4,128)(2,1)} %copy.58), calls=%async_computation.2 | async-start | bytes 2097152 | tf_op jit(solution)/shard_map/all_to_all | solution.py:97
  1035.4 0.1 convert_element_type.92
  1035.5 0.1 convolution_convert_fusion.1
  1035.6 0.6 reshape.341
  1036.2 0.3 copy.60
  1036.5 21.5 %all-to-all-done.2 = bf16[4,16,8192]{2,0,1:T(4,128)(2,1)S(1)} async-done(((bf16[4,16,8192]{2,0,1:T(4,128)(2,1)}), bf16[4,16,8192]{2,0,1:T(4,128)(2,1)S(1)}, u32[]{:S(2)}, u32[]{:S(2)}) %all-to-all-start.2) | async-done | bytes 1048608 | tf_op jit(solution)/shard_map/all_to_all | solution.py:97
  1057.9 0.3 reshape.346
  1058.2 0.4 fusion.1
  1058.6 0.8 copy.61
  1059.5 30.0 %all_to_all.40 = bf16[4,16,8192]{2,0,1:T(4,128)(2,1)S(1)} all-to-all(bf16[4,16,8192]{2,0,1:T(4,128)(2,1)S(1)} %copy.61), channel_id=1, replica_groups=mesh['freq'=16,'panel'=2] {'freq'}, dimensions={1} | all-to-all | bytes 2097152 | tf_op jit(solution)/shard_map/all_to_all | solution.py:102
  1089.5 0.6 copy.62
  1090.1 1.3 reshape.342
  (8 shorter events, 0.1 us)
Async XLA Ops:
  45.6 323.7 %all-to-all-start = ((bf16[4,16,131072]{2,0,1:T(4,128)(2,1)}), bf16[4,16,131072]{2,0,1:T(4,128)(2,1)}, u32[]{:S(2)}, u32[]{:S(2)}) async-start(bf16[4,16,131072]{2,0,1:T(4,128)(2,1)} %copy.53), calls=%async_computation | async-start | bytes 33554432 | tf_op jit(solution)/shard_map/all_to_all | solution.py:64
  417.9 73.6 %copy-start.4 = (s32[32]{0:T(128)S(1)}, s32[32]{0:T(128)}, u32[]{:S(2)}) copy-start(s32[32]{0:T(128)} %param.4) | copy-start | bytes 388
  417.9 73.6 %copy-start.5 = (s32[32]{0:T(128)S(1)}, s32[32]{0:T(128)}, u32[]{:S(2)}) copy-start(s32[32]{0:T(128)} %param.5) | copy-start | bytes 388
  417.9 385.9 %all-to-all-start.1 = ((bf16[4,16,131072]{2,0,1:T(4,128)(2,1)}), bf16[4,16,131072]{2,0,1:T(4,128)(2,1)}, u32[]{:S(2)}, u32[]{:S(2)}) async-start(bf16[4,16,131072]{2,0,1:T(4,128)(2,1)} %copy.54), calls=%async_computation.1 | async-start | bytes 33554432 | tf_op jit(solution)/shard_map/all_to_all | solution.py:68
  491.1 456.6 %all-gather.2.cloned.1.call-start = ((), (), s32[]{:S(2)}) async-start(), calls=%async_computation.4 | async-start | bytes 3145728 | tf_op jit(solution)/shard_map/all_gather | solution.py:80
  949.0 2.8 copy-start.3
  950.8 2.5 copy-start.1
  953.4 2.4 copy-start
  953.4 3.5 copy-start.2
  962.7 95.3 %all-to-all-start.2 = ((bf16[4,16,8192]{2,0,1:T(4,128)(2,1)}), bf16[4,16,8192]{2,0,1:T(4,128)(2,1)S(1)}, u32[]{:S(2)}, u32[]{:S(2)}) async-start(bf16[4,16,8192]{2,0,1:T(4,128)(2,1)} %copy.58), calls=%async_computation.2 | async-start | bytes 2097152 | tf_op jit(solution)/shard_map/all_to_all | solution.py:97
Sparse Core Ops, SparseCore 0:
  842.5 77.6 all-gather.1
where the time goes:
time: 1100 us
  waiting for transfers between devices  648 us (59%)
  local copies, waits for them, and re-layouts  231 us (21%)
  starting transfers between devices  154 us (14%)
  blocking collectives  30 us (3%)
  matrix products  16.8 us (2%)
  between operations  13.6 us (1%)
    all_to_all x1, waiting for transfers between devices, body(): lax.all_to_all(outgoing_time, 'freq', split_axis=1, concat_axis=0, tiled=...  315 us
    all_to_all x1, waiting for transfers between devices, body(): lax.all_to_all(spectra, 'freq', split_axis=1, concat_axis=1, tiled=True)  312 us
    slice x1, local copies, waits for them, and re-layouts, body(): stacked_left = jnp.concatenate([left_block[0], left_block[1]], axis=1)  86.1 us
    all_to_all x1, starting transfers between devices, body(): lax.all_to_all(spectra, 'freq', split_axis=1, concat_axis=1, tiled=True)  73.2 us
    all_to_all x1, starting transfers between devices, body(): lax.all_to_all(outgoing_freq, 'freq', split_axis=1, concat_axis=0, tiled=...  72.7 us
    reshape x2, local copies, waits for them, and re-layouts, body(): outgoing_time = shot_gathers.reshape(time_local, owners, trace_width)  39.1 us
    all_to_all x1, blocking collectives, body(): lax.all_to_all(traces.astype(jnp.bfloat16), 'freq', split_axis=1, concat_...  30 us
    convert_element_type x1, local copies, waits for them, and re-layouts, body(): spectra = jnp.einsum('qot,tw->qow', forward_rows, series, preferred_eleme...  22.1 us
  transfers between devices with their start and end apart: 4, of which 3 were waited for; matrix products, arithmetic and copies ran while one was open for 10% of the time, Pallas kernels for 0%

commit v1 on v0

--- a/solution.py
+++ b/solution.py
@@ -1,14 +1,127 @@
+import functools
 import math
 
 import jax
 import jax.numpy as jnp
 from jax import lax
+from jax.experimental import pallas as pl
+from jax.experimental.pallas import tpu as pltpu
 from jax.sharding import PartitionSpec as P
 
 SW = 128
 BLOCK = 128
+TAPER = 64
 F_DEV = 2
-TAPER = 64
+RESPONSE_LIMIT = 2**26
+
+
+def taper_weights(aperture, taper_level, surface_points):
+    ends = aperture * BLOCK
+    ramp = jnp.minimum(TAPER * (1 + taper_level), ends)
+    begins = ends - ramp
+    offset = (surface_points - begins + 1).astype(jnp.float32)
+    wave = jnp.cos(0.5 * math.pi * offset / (ramp + 1).astype(jnp.float32))
+    inside = jnp.where(surface_points < ends, wave * wave, jnp.zeros_like(wave))
+    return jnp.where(surface_points < begins, jnp.ones_like(wave), inside)
+
+
+def convolve_kernel(j_ref, d_ref, cur_ref, prev_ref, out_ref, pairs):
+    steps, rows, points = d_ref.shape
+
+    def slab(m):
+        part = cur_ref[:, m] if m >= 0 else prev_ref[:, steps + m]
+        return part.reshape(points, SW)
+
+    for m in range(1 - steps, steps - 1):
+        at = m + steps - 1
+        pairs[at, :, :SW] = slab(m)
+        pairs[at, :, SW:] = slab(m + 1)
+    tile = 256
+
+    @pl.loop(0, rows // tile)
+    def _(r):
+        here = pl.ds(pl.multiple_of(r * tile, tile), tile)
+        for q in range(0, steps, 2):
+            total = None
+            for i in range(steps):
+                term = jnp.dot(
+                    d_ref[i, here, :], pairs[q - i + steps - 1], preferred_element_type=jnp.float32
+                )
+                total = term if total is None else total + term
+            out_ref[q, here, :] = total[:, :SW].astype(jnp.bfloat16)
+            out_ref[q + 1, here, :] = total[:, SW:].astype(jnp.bfloat16)
+
+
+def convolve(index, data, response):
+    steps, rows, points = data.shape
+    groups, times, each, _ = response.shape
+    count = times // steps
+    return pl.pallas_call(
+        convolve_kernel,
+        grid_spec=pltpu.PrefetchScalarGridSpec(
+            num_scalar_prefetch=1,
+            grid=(count,),
+            in_specs=[
+                pl.BlockSpec((steps, rows, points), lambda b, j: (0, 0, 0), pipeline_mode=pl.Buffered(1)),
+                pl.BlockSpec((groups, steps, each, SW), lambda b, j: (0, b, 0, 0)),
+                pl.BlockSpec(
+                    (groups, steps, each, SW), lambda b, j: (0, lax.rem(b + count - 1, count), 0, 0)
+                ),
+            ],
+            out_specs=pl.BlockSpec(
+                (steps, rows, SW), lambda b, j: (lax.rem(b + j[0], count), 0, 0)
+            ),
+            scratch_shapes=[pltpu.VMEM((2 * steps - 2, points, 2 * SW), jnp.bfloat16)],
+        ),
+        out_shape=jax.ShapeDtypeStruct((times, rows, SW), jnp.bfloat16),
+        compiler_params=pltpu.CompilerParams(vmem_limit_bytes=56 * 2**20),
+        cost_estimate=pl.CostEstimate(
+            flops=2 * steps * rows * points * SW * times,
+            bytes_accessed=2 * (steps * rows * points + 2 * times * points * SW + times * rows * SW),
+            transcendentals=0,
+        ),
+    )(index, data, response, response)
+
+
+def angles(freq_total, time_total):
+    bins = jnp.arange(freq_total, dtype=jnp.int32) + 1
+    times = jnp.arange(time_total, dtype=jnp.int32)
+    phase = bins[:, None] * times[None, :] % time_total
+    return phase.astype(jnp.float32) * (2.0 * math.pi / time_total)
+
+
+def window_response(window, aperture_blocks, taper_index, points, points_total):
+    time_total, count, _ = window.shape
+    freq_total = aperture_blocks.shape[0]
+    angle = angles(freq_total, time_total)
+    forward = jnp.stack([jnp.cos(angle), -jnp.sin(angle)], axis=1) * (1.0 / math.sqrt(time_total))
+    spectra = jnp.einsum(
+        "fct,tks->fcks", forward.astype(jnp.bfloat16), window, preferred_element_type=jnp.float32
+    ).astype(jnp.bfloat16)
+    weights = taper_weights(aperture_blocks[:, None], taper_index[:, None], points[None, :])
+    tapered = (weights[:, None, :, None] * spectra.astype(jnp.float32)).astype(jnp.bfloat16)
+    scale = -1.0 / math.sqrt(time_total * points_total * freq_total)
+    back = jnp.stack([jnp.cos(angle), -jnp.sin(angle)], axis=1) * scale
+    return jnp.einsum(
+        "fct,fcks->tks", back, tapered.astype(jnp.float32), precision=lax.Precision.HIGHEST
+    ).astype(jnp.bfloat16)
+
+
+def body(shot_gathers, aperture_blocks, taper_index):
+    steps, rows, points_total = shot_gathers.shape
+    owners = lax.axis_size("freq")
+    if 2 * steps * owners * points_total * SW > RESPONSE_LIMIT:
+        return frequency_body(shot_gathers, aperture_blocks, taper_index)
+    index = lax.axis_index("freq").astype(jnp.int32)
+    each = rows // owners
+    window = lax.all_to_all(
+        shot_gathers[:, :, :SW], "freq", split_axis=1, concat_axis=0, tiled=True
+    )
+    points = lax.axis_index("panel") * rows + index * each + jnp.arange(each, dtype=jnp.int32)
+    response = window_response(window, aperture_blocks, taper_index, points, points_total)
+    response = lax.all_gather(response, ("panel", "freq"), axis=0, tiled=False)
+    partial = convolve(index[None], shot_gathers, response)
+    return lax.psum_scatter(partial, "freq", scatter_dimension=0, tiled=True)
 
 
 def transform_tables(freq_total, time_total):
@@ -24,17 +137,7 @@
     return (forward, inverse)
 
 
-def taper_weights(aperture, taper_level, surface_points):
-    ends = aperture * BLOCK
-    ramp = jnp.minimum(TAPER * (1 + taper_level), ends)
-    begins = ends - ramp
-    offset = (surface_points - begins + 1).astype(jnp.float32)
-    wave = jnp.cos(0.5 * math.pi * offset / (ramp + 1).astype(jnp.float32))
-    inside = jnp.where(surface_points < ends, wave * wave, jnp.zeros_like(wave))
-    return jnp.where(surface_points < begins, jnp.ones_like(wave), inside)
-
-
-def body(shot_gathers, aperture_blocks, taper_index):
+def frequency_body(shot_gathers, aperture_blocks, taper_index):
     time_local, rows_local, points_total = shot_gathers.shape
     owners = lax.axis_size("freq")
     slot_count = 2 * F_DEV

time: 1100 us -> 802 us (0.73)
  local copies, waits for them, and re-layouts: 231 us -> 32.6 us
  Pallas kernels: 0 us -> 171 us
  starting transfers between devices: 154 us -> 8.4 us
  waiting for transfers between devices: 648 us -> 569 us
  blocking collectives: 30 us -> 0 us
  matrix products: 16.8 us -> 2.99 us
    all_to_all x3 -> x1, waiting for transfers between devices: 648 us -> 24 us  [body(): lax.all_to_all(shot_gathers[:, :, :SW], 'freq', split_axis=1, concat_axis...]
    reduce_scatter x0 -> x1, waiting for transfers between devices: none -> 346 us  [body(): return lax.psum_scatter(partial, 'freq', scatter_dimension=0, tiled=True)]
    all_gather x1, waiting for transfers between devices: 0.01 us -> 199 us  [body(): response = lax.all_gather(response, ('panel', 'freq'), axis=0, tiled=False)]
    pallas_call x0 -> x1, Pallas kernels: none -> 171 us  [convolve(): pl.pallas_call(convolve_kernel, grid_spec=pltpu.PrefetchScalarGridSpec(nu...]
    all_to_all x3 -> x1, starting transfers between devices: 154 us -> 8.31 us  [body(): lax.all_to_all(shot_gathers[:, :, :SW], 'freq', split_axis=1, concat_axis...]
    slice x2, local copies, waits for them, and re-layouts: 87.3 us -> 1.22 us  [body(): shot_gathers[:, :, :SW]]
    reshape x7 -> x0, local copies, waits for them, and re-layouts: 58.3 us -> none  [the longest x2 39.1 us: body(): outgoing_time = shot_gathers.reshape(time_local, owners, trace_width)]
    squeeze x7 -> x0, local copies, waits for them, and re-layouts: 36.4 us -> none  [the longest x4 19.3 us: body(): stacked_left = jnp.concatenate([left_block[0], left_block[1]], axis=1)]
  transfers between devices with their start and end apart: 4 -> 3, of which waited for: 3 -> 3; matrix products, arithmetic and copies ran while one was open for 10% -> 0% of each run, Pallas kernels for 0% -> 0%
where the time goes in v1:
time: 802 us; the launch traced here: 798 us
  waiting for transfers between devices  569 us (71%)
  Pallas kernels  171 us (21%)
  local copies, waits for them, and re-layouts  32.6 us (4%)
  between operations  13.5 us (2%)
  starting transfers between devices  8.4 us (1%)
    reduce_scatter x1, waiting for transfers between devices, body(): return lax.psum_scatter(partial, 'freq', scatter_dimension=0, tiled=True)  346 us
    all_gather x1, waiting for transfers between devices, body(): response = lax.all_gather(response, ('panel', 'freq'), axis=0, tiled=False)  199 us
    pallas_call x1, Pallas kernels, convolve(): pl.pallas_call(convolve_kernel, grid_spec=pltpu.PrefetchScalarGridSpec(nu...  171 us
    all_gather x1, local copies, waits for them, and re-layouts, body(): response = lax.all_gather(response, ('panel', 'freq'), axis=0, tiled=False)  29.4 us
    all_to_all x1, waiting for transfers between devices, body(): lax.all_to_all(shot_gathers[:, :, :SW], 'freq', split_axis=1, concat_axis...  24 us
  transfers between devices with their start and end apart: 3, of which 3 were waited for; matrix products, arithmetic and copies ran while one was open for 0% of the time, Pallas kernels for 0%

profile of v1, /device:TPU:0, one launch (start us, length us, event | category | flops | bytes accessed | tf_op | source)
XLA Modules:
  0.0 798.1 jit_solution(939146295263682566)
XLA Ops:
  6.5 0.0 slice-start
  6.5 1.2 slice-done
  7.8 0.0 copy-start
  7.8 0.0 copy-start.1
  7.8 1.8 copy.18
  9.5 8.3 %all-to-all-start = ((bf16[4,1024,128]{2,0,1:T(4,128)(2,1)}), bf16[4,1024,128]{2,0,1:T(4,128)(2,1)S(1)}, u32[]{:S(2)}, u32[]{:S(2)}) async-start(bf16[4,1024,128]{2,0,1:T(4,128)(2,1)} %copy.18), calls=%async_computation | async-start | bytes 2097152 | tf_op jit(solution)/shard_map/all_to_all | solution.py:117
  17.9 0.0 all-gather.3.cloned.1.call-start
  17.9 0.0 copy-done
  18.0 0.0 copy-done.1
  18.0 0.2 fusion.13
  18.1 0.2 select_select_fusion
  18.3 24.0 %all-to-all-done = bf16[4,1024,128]{2,0,1:T(4,128)(2,1)S(1)} async-done(((bf16[4,1024,128]{2,0,1:T(4,128)(2,1)}), bf16[4,1024,128]{2,0,1:T(4,128)(2,1)S(1)}, u32[]{:S(2)}, u32[]{:S(2)}) %all-to-all-start) | async-done | bytes 1048608 | tf_op jit(solution)/shard_map/all_to_all | solution.py:117
  42.3 0.1 copy.10
  42.5 0.1 copy.11
  42.5 1.0 multiply_convert_fusion
  43.5 2.0 bitcast_convert_fusion
  45.5 0.0 all-gather.3.cloned.1.call-update
  45.6 0.0 reduce-scatter.2.cloned.1.call-start
  45.6 199.3 %all-gather.3.cloned.1.call-done = bf16[2048,64,128]{2,0,1:T(8,128)(2,1)} async-done(((bf16[64,64,128]{2,0,1:T(8,128)(2,1)}), bf16[2048,64,128]{2,0,1:T(8,128)(2,1)}) %all-gather.3.cloned.1.call-update) | async-done | bytes 33554448 | tf_op jit(solution)/shard_map/all_gather | solution.py:122
  244.9 29.4 %copy.13 = bf16[2048,64,128]{2,1,0:T(8,128)(2,1)} copy(bf16[2048,64,128]{2,0,1:T(8,128)(2,1)} %all-gather.3.cloned.1.call-done) | data formatting | bytes 67108864 | tf_op jit(solution)/shard_map/all_gather | solution.py:122
  274.3 171.3 %shard_map.37 = bf16[64,1024,128]{2,1,0:T(8,128)(2,1)} custom-call(s32[1]{0:T(128)} %bitcast.j_ref, bf16[4,1024,2048]{2,1,0:T(8,128)(2,1)} %d_ref.1, bf16[32,64,64,128]{3,2,1,0:T(8,128)(2,1)} %bitcast.18, bf16[32,64,64,128]{3,2,1,0:T(8,128)(2,1)} %bitcast.19), custom_call_target="tpu_custom_call" | custom-call | flops 137438953472 | bytes 100663296 | tf_op jit(solution)/shard_map/pallas_call | solution.py:59
  445.6 0.0 reduce-scatter.2.cloned.1.call-update
  445.6 345.6 %reduce-scatter.2.cloned.1.call-done = bf16[4,1024,128]{2,1,0:T(8,128)(2,1)} async-done(((bf16[64,1024,128]{2,1,0:T(8,128)(2,1)}), bf16[4,1024,128]{2,1,0:T(8,128)(2,1)}) %reduce-scatter.2.cloned.1.call-update) | async-done | bytes 1048592 | tf_op jit(solution)/shard_map/reduce_scatter | solution.py:124
  (3 shorter events, 0.0 us)
Async XLA Ops:
  6.5 1.2 slice-start
  7.8 10.2 %copy-start = (s32[32]{0:T(128)S(1)}, s32[32]{0:T(128)}, u32[]{:S(2)}) copy-start(s32[32]{0:T(128)} %param.5) | copy-start | bytes 388
  7.8 10.2 %copy-start.1 = (s32[32]{0:T(128)S(1)}, s32[32]{0:T(128)}, u32[]{:S(2)}) copy-start(s32[32]{0:T(128)} %param.4) | copy-start | bytes 388
  9.5 32.8 %all-to-all-start = ((bf16[4,1024,128]{2,0,1:T(4,128)(2,1)}), bf16[4,1024,128]{2,0,1:T(4,128)(2,1)S(1)}, u32[]{:S(2)}, u32[]{:S(2)}) async-start(bf16[4,1024,128]{2,0,1:T(4,128)(2,1)} %copy.18), calls=%async_computation | async-start | bytes 2097152 | tf_op jit(solution)/shard_map/all_to_all | solution.py:117
  17.9 227.0 %all-gather.3.cloned.1.call-start = ((), (), s32[]{:S(2)}) async-start(), calls=%async_computation.3 | async-start | bytes 34603008 | tf_op jit(solution)/shard_map/all_gather | solution.py:122
  45.6 745.7 %reduce-scatter.2.cloned.1.call-start = ((), (), s32[]{:S(2)}) async-start(), calls=%async_computation.2 | async-start | bytes 17825792 | tf_op jit(solution)/shard_map/reduce_scatter | solution.py:124
Sparse Core Ops, SparseCore 0:
  45.7 199.1 all-gather.2
  445.7 345.4 reduce-scatter.1

commit v2 on v1

--- a/solution.py
+++ b/solution.py
@@ -25,62 +25,186 @@
     return jnp.where(surface_points < begins, jnp.ones_like(wave), inside)
 
 
-def convolve_kernel(j_ref, d_ref, cur_ref, prev_ref, out_ref, pairs):
-    steps, rows, points = d_ref.shape
-
-    def slab(m):
-        part = cur_ref[:, m] if m >= 0 else prev_ref[:, steps + m]
-        return part.reshape(points, SW)
-
-    for m in range(1 - steps, steps - 1):
-        at = m + steps - 1
-        pairs[at, :, :SW] = slab(m)
-        pairs[at, :, SW:] = slab(m + 1)
+def ring_place(index, levels):
+    z, y, x = index // 4, index // 2 % 2, index % 2
+    column = 2 * y + x + y - 2 * x * y
+    return column * levels + z + column % 2 * (levels - 1 - 2 * z)
+
+
+def ring_index(place, levels):
+    column, along = place // levels, place % levels
+    z = along + column % 2 * (levels - 1 - 2 * along)
+    y = column // 2
+    return 4 * z + 2 * y + (column + y) % 2
+
+
+def convolve_kernel(
+    owners, d_hbm, h_hbm, out_ref, data, pairs, total_ref, send, from_left, from_right,
+    data_sem, pair_sem, send_sem, left_sem, right_sem,
+):
+    steps, rows, points = d_hbm.shape
+    times = steps * owners
+    groups, each = h_hbm.shape[0], h_hbm.shape[2]
+    levels = owners // 4
+    half = owners // 2
     tile = 256
-
-    @pl.loop(0, rows // tile)
-    def _(r):
-        here = pl.ds(pl.multiple_of(r * tile, tile), tile)
-        for q in range(0, steps, 2):
-            total = None
-            for i in range(steps):
-                term = jnp.dot(
-                    d_ref[i, here, :], pairs[q - i + steps - 1], preferred_element_type=jnp.float32
+    me = lax.axis_index("freq")
+    place = ring_place(me, levels)
+    right = ring_index((place + 1) % owners, levels)
+    left = ring_index((place + owners - 1) % owners, levels)
+
+    barrier = pltpu.get_barrier_semaphore()
+    for neighbour in (left, right):
+        pl.semaphore_signal(
+            barrier, inc=1, device_id={"freq": neighbour}, device_id_type=pl.DeviceIdType.MESH
+        )
+
+    def pair_copies(buffer, base):
+        copies = []
+        for at in range(2 * steps - 2):
+            for side in range(2):
+                tau = (base + at + side + times + 1 - steps) % times
+                copies.append(
+                    pltpu.make_async_copy(
+                        h_hbm.at[:, tau],
+                        pairs.at[buffer, at, :, :, pl.ds(side * SW, SW)],
+                        pair_sem.at[buffer, 2 * at + side],
+                    )
                 )
-                total = term if total is None else total + term
-            out_ref[q, here, :] = total[:, :SW].astype(jnp.bfloat16)
-            out_ref[q + 1, here, :] = total[:, SW:].astype(jnp.bfloat16)
-
-
-def convolve(index, data, response):
+        return copies
+
+    def fetch(buffer, distance):
+        owner = ring_index((place + distance + owners) % owners, levels)
+        for copy in pair_copies(buffer, steps * ((owner - me + owners) % owners)):
+            copy.start()
+
+    def compute(buffer):
+        for copy in pair_copies(buffer, 0):
+            copy.wait()
+
+        @pl.loop(0, rows // tile)
+        def _(r):
+            here = pl.ds(pl.multiple_of(r * tile, tile), tile)
+            for q in range(0, steps, 2):
+                total = None
+                for i in range(steps):
+                    term = jnp.dot(
+                        data[i, here, :],
+                        pairs[buffer, q - i + steps - 1].reshape(points, 2 * SW),
+                        preferred_element_type=jnp.float32,
+                    )
+                    total = term if total is None else total + term
+                total_ref[q, here, :] = total[:, :SW]
+                total_ref[q + 1, here, :] = total[:, SW:]
+
+    def store(target, terms):
+        @pl.loop(0, rows // tile)
+        def _(r):
+            here = pl.ds(pl.multiple_of(r * tile, tile), tile)
+            for q in range(steps):
+                value = total_ref[q, here, :]
+                for term in terms:
+                    value = value + term[q, here, :].astype(jnp.float32)
+                target[q, here, :] = value.astype(jnp.bfloat16)
+
+    def sending(way, distance):
+        landing, sem, to = ((from_left, left_sem, right), (from_right, right_sem, left))[way]
+        return pltpu.make_async_remote_copy(
+            src_ref=send.at[way, distance % 2],
+            dst_ref=landing.at[distance - 1],
+            send_sem=send_sem.at[way, distance % 2],
+            recv_sem=sem.at[distance - 1],
+            device_id={"freq": to},
+            device_id_type=pl.DeviceIdType.MESH,
+        )
+
+    load = pltpu.make_async_copy(d_hbm, data, data_sem)
+    load.start()
+    fetch(0, half)
+    fetch(1, 1 - half)
+    load.wait()
+
+    compute(0)
+    fetch(0, half - 1)
+    store(send.at[0, half % 2], [])
+    pl.semaphore_wait(barrier, 2)
+    sending(0, half).start()
+
+    @pl.loop(0, half - 1)
+    def _(n):
+        distance = half - 1 - n
+        compute(1)
+        fetch(1, 1 - distance)
+
+        @pl.when(n >= 2)
+        def _():
+            sending(1, distance + 2).wait_send()
+
+        @pl.when(n >= 1)
+        def _():
+            sending(1, distance + 1).wait_recv()
+            store(send.at[1, distance % 2], [from_right.at[distance]])
+
+        @pl.when(n == 0)
+        def _():
+            store(send.at[1, distance % 2], [])
+
+        sending(1, distance).start()
+        compute(0)
+
+        @pl.when(distance > 1)
+        def _():
+            fetch(0, distance - 1)
+
+        @pl.when(n >= 1)
+        def _():
+            sending(0, distance + 2).wait_send()
+
+        sending(0, distance + 1).wait_recv()
+        store(send.at[0, distance % 2], [from_left.at[distance]])
+        sending(0, distance).start()
+
+    compute(1)
+    sending(0, 1).wait_recv()
+    sending(1, 1).wait_recv()
+    store(out_ref, [from_left.at[0], from_right.at[0]])
+    for way in range(2):
+        for distance in (2, 1):
+            sending(way, distance).wait_send()
+
+
+def convolve(data, response, owners):
     steps, rows, points = data.shape
     groups, times, each, _ = response.shape
-    count = times // steps
+    half = owners // 2
+    block = (steps, rows, SW)
     return pl.pallas_call(
-        convolve_kernel,
-        grid_spec=pltpu.PrefetchScalarGridSpec(
-            num_scalar_prefetch=1,
-            grid=(count,),
-            in_specs=[
-                pl.BlockSpec((steps, rows, points), lambda b, j: (0, 0, 0), pipeline_mode=pl.Buffered(1)),
-                pl.BlockSpec((groups, steps, each, SW), lambda b, j: (0, b, 0, 0)),
-                pl.BlockSpec(
-                    (groups, steps, each, SW), lambda b, j: (0, lax.rem(b + count - 1, count), 0, 0)
-                ),
-            ],
-            out_specs=pl.BlockSpec(
-                (steps, rows, SW), lambda b, j: (lax.rem(b + j[0], count), 0, 0)
-            ),
-            scratch_shapes=[pltpu.VMEM((2 * steps - 2, points, 2 * SW), jnp.bfloat16)],
+        functools.partial(convolve_kernel, owners),
+        in_specs=[pl.BlockSpec(memory_space=pl.ANY)] * 2,
+        out_specs=pl.BlockSpec(memory_space=pltpu.VMEM),
+        out_shape=jax.ShapeDtypeStruct(block, jnp.bfloat16),
+        scratch_shapes=[
+            pltpu.VMEM(data.shape, jnp.bfloat16),
+            pltpu.VMEM((2, 2 * steps - 2, groups, each, 2 * SW), jnp.bfloat16),
+            pltpu.VMEM(block, jnp.float32),
+            pltpu.VMEM((2, 2) + block, jnp.bfloat16),
+            pltpu.VMEM((half,) + block, jnp.bfloat16),
+            pltpu.VMEM((half - 1,) + block, jnp.bfloat16),
+            pltpu.SemaphoreType.DMA,
+            pltpu.SemaphoreType.DMA((2, 4 * steps - 4)),
+            pltpu.SemaphoreType.DMA((2, 2)),
+            pltpu.SemaphoreType.DMA((half,)),
+            pltpu.SemaphoreType.DMA((half - 1,)),
+        ],
+        compiler_params=pltpu.CompilerParams(
+            vmem_limit_bytes=58 * 2**20, collective_id=0, has_side_effects=True
         ),
-        out_shape=jax.ShapeDtypeStruct((times, rows, SW), jnp.bfloat16),
-        compiler_params=pltpu.CompilerParams(vmem_limit_bytes=56 * 2**20),
         cost_estimate=pl.CostEstimate(
             flops=2 * steps * rows * points * SW * times,
-            bytes_accessed=2 * (steps * rows * points + 2 * times * points * SW + times * rows * SW),
+            bytes_accessed=2 * (steps * rows * points + 3 * times * points * SW),
             transcendentals=0,
         ),
-    )(index, data, response, response)
+    )(data, response)
 
 
 def angles(freq_total, time_total):
@@ -112,16 +236,17 @@
     owners = lax.axis_size("freq")
     if 2 * steps * owners * points_total * SW > RESPONSE_LIMIT:
         return frequency_body(shot_gathers, aperture_blocks, taper_index)
-    index = lax.axis_index("freq").astype(jnp.int32)
+    index = lax.axis_index("freq")
     each = rows // owners
     window = lax.all_to_all(
         shot_gathers[:, :, :SW], "freq", split_axis=1, concat_axis=0, tiled=True
     )
     points = lax.axis_index("panel") * rows + index * each + jnp.arange(each, dtype=jnp.int32)
     response = window_response(window, aperture_blocks, taper_index, points, points_total)
-    response = lax.all_gather(response, ("panel", "freq"), axis=0, tiled=False)
-    partial = convolve(index[None], shot_gathers, response)
-    return lax.psum_scatter(partial, "freq", scatter_dimension=0, tiled=True)
+    response = lax.all_gather(
+        response.reshape(-1, SW), ("panel", "freq"), axis=0, tiled=True
+    ).reshape(-1, steps * owners, each, SW)
+    return convolve(shot_gathers, response, owners)
 
 
 def transform_tables(freq_total, time_total):

time: 802 us -> 455 us (0.57)
  waiting for transfers between devices: 569 us -> 219 us
  Pallas kernels: 171 us -> 204 us
  local copies, waits for them, and re-layouts: 32.6 us -> 7.15 us
    reduce_scatter x1 -> x0, waiting for transfers between devices: 346 us -> none  [body(): return lax.psum_scatter(partial, 'freq', scatter_dimension=0, tiled=True)]
    pallas_call x1, Pallas kernels: 171 us -> 204 us  [convolve(): pl.pallas_call(functools.partial(convolve_kernel, owners), in_specs=[pl.B...]
    all_gather x1 -> x0, local copies, waits for them, and re-layouts: 29.4 us -> none  [body(): response = lax.all_gather(response, ('panel', 'freq'), axis=0, tiled=False)]
  transfers between devices with their start and end apart: 3 -> 2, of which waited for: 3 -> 2; matrix products, arithmetic and copies ran while one was open for 0% -> 0% of each run, Pallas kernels for 0% -> 0%
where the time goes in v2:
time: 455 us
  waiting for transfers between devices  219 us (48%)
  Pallas kernels  204 us (45%)
  between operations  13.5 us (3%)
  starting transfers between devices  8.35 us (2%)
  local copies, waits for them, and re-layouts  7.15 us (2%)
    pallas_call x1, Pallas kernels, convolve(): pl.pallas_call(functools.partial(convolve_kernel, owners), in_specs=[pl.B...  204 us
    all_gather x1, waiting for transfers between devices, body(): lax.all_gather(response.reshape(-1, SW), ('panel', 'freq'), axis=0, tiled...  195 us
    all_to_all x1, waiting for transfers between devices, body(): lax.all_to_all(shot_gathers[:, :, :SW], 'freq', split_axis=1, concat_axis...  24 us
  transfers between devices with their start and end apart: 2, of which 2 were waited for; matrix products, arithmetic and copies ran while one was open for 0% of the time, Pallas kernels for 0%

profile of v2, /device:TPU:0, one launch (start us, length us, event | category | flops | bytes accessed | tf_op | source)
XLA Modules:
  0.0 454.7 jit_solution(11380084017904446500)
XLA Ops:
  6.5 0.0 slice-start
  6.5 1.2 slice-done
  7.8 0.0 copy-start
  7.8 0.0 copy-start.1
  7.8 1.8 copy.17
  9.5 8.3 %all-to-all-start = ((bf16[4,1024,128]{2,0,1:T(4,128)(2,1)}), bf16[4,1024,128]{2,0,1:T(4,128)(2,1)S(1)}, u32[]{:S(2)}, u32[]{:S(2)}) async-start(bf16[4,1024,128]{2,0,1:T(4,128)(2,1)} %copy.17), calls=%async_computation | async-start | bytes 2097152 | tf_op jit(solution)/shard_map/all_to_all | solution.py:241
  17.9 0.0 all-gather.2.cloned.1.call-start
  17.9 0.0 copy-done
  18.0 0.0 copy-done.1
  18.0 0.2 fusion.13
  18.1 0.2 select_select_fusion
  18.3 24.0 %all-to-all-done = bf16[4,1024,128]{2,0,1:T(4,128)(2,1)S(1)} async-done(((bf16[4,1024,128]{2,0,1:T(4,128)(2,1)}), bf16[4,1024,128]{2,0,1:T(4,128)(2,1)S(1)}, u32[]{:S(2)}, u32[]{:S(2)}) %all-to-all-start) | async-done | bytes 1048608 | tf_op jit(solution)/shard_map/all_to_all | solution.py:241
  42.3 0.1 copy.9
  42.5 0.1 copy.10
  42.5 1.0 multiply_convert_fusion
  43.5 1.1 bitcast_convert_fusion
  44.6 1.6 copy.12
  46.2 0.0 all-gather.2.cloned.1.call-update
  46.3 195.1 %all-gather.2.cloned.1.call-done = bf16[131072,128]{1,0:T(8,128)(2,1)} async-done(((bf16[4096,128]{1,0:T(8,128)(2,1)}), bf16[131072,128]{1,0:T(8,128)(2,1)}) %all-gather.2.cloned.1.call-update) | async-done | bytes 33554448 | tf_op jit(solution)/shard_map/all_gather | solution.py:246
  241.4 204.2 %shard_map.37 = bf16[4,1024,128]{2,1,0:T(8,128)(2,1)} custom-call(bf16[4,1024,2048]{2,1,0:T(8,128)(2,1)} %d_hbm.1, bf16[32,64,64,128]{3,2,1,0:T(8,128)(2,1)} %bitcast.21), custom_call_target="tpu_custom_call" | custom-call | flops 137438953472 | bytes 117440512 | tf_op jit(solution)/shard_map/pallas_call | solution.py:181
  445.6 2.3 copy.21
  (3 shorter events, 0.0 us)
Async XLA Ops:
  6.5 1.2 slice-start
  7.8 10.2 %copy-start = (s32[32]{0:T(128)S(1)}, s32[32]{0:T(128)}, u32[]{:S(2)}) copy-start(s32[32]{0:T(128)} %param.5) | copy-start | bytes 388
  7.8 10.2 %copy-start.1 = (s32[32]{0:T(128)S(1)}, s32[32]{0:T(128)}, u32[]{:S(2)}) copy-start(s32[32]{0:T(128)} %param.4) | copy-start | bytes 388
  9.5 32.8 %all-to-all-start = ((bf16[4,1024,128]{2,0,1:T(4,128)(2,1)}), bf16[4,1024,128]{2,0,1:T(4,128)(2,1)S(1)}, u32[]{:S(2)}, u32[]{:S(2)}) async-start(bf16[4,1024,128]{2,0,1:T(4,128)(2,1)} %copy.17), calls=%async_computation | async-start | bytes 2097152 | tf_op jit(solution)/shard_map/all_to_all | solution.py:241
  17.9 223.5 %all-gather.2.cloned.1.call-start = ((), (), s32[]{:S(2)}) async-start(), calls=%async_computation.1 | async-start | bytes 34603008 | tf_op jit(solution)/shard_map/all_gather | solution.py:246
Sparse Core Ops, SparseCore 0:
  46.4 194.9 all-gather.1

commit v3 on v2

--- a/solution.py
+++ b/solution.py
@@ -243,9 +243,9 @@
     )
     points = lax.axis_index("panel") * rows + index * each + jnp.arange(each, dtype=jnp.int32)
     response = window_response(window, aperture_blocks, taper_index, points, points_total)
-    response = lax.all_gather(
-        response.reshape(-1, SW), ("panel", "freq"), axis=0, tiled=True
-    ).reshape(-1, steps * owners, each, SW)
+    response = lax.all_gather(response.reshape(-1, SW), "freq", axis=0, tiled=True)
+    response = lax.all_gather(response, "panel", axis=0, tiled=True)
+    response = response.reshape(-1, steps * owners, each, SW)
     return convolve(shot_gathers, response, owners)
 
 

time: 455 us -> 506 us (1.11)
  waiting for transfers between devices: 219 us -> 267 us
    all_gather x1 -> x2, waiting for transfers between devices: 195 us -> 243 us  [the longest x1 192 us: body(): lax.all_gather(response.reshape(-1, SW), 'freq', axis=0, tiled=True)]
  transfers between devices with their start and end apart: 2 -> 3, of which waited for: 2 -> 3; matrix products, arithmetic and copies ran while one was open for 0% -> 0% of each run, Pallas kernels for 0% -> 0%
where the time goes in v3:
time: 506 us; the launch traced here: 505 us
  waiting for transfers between devices  267 us (53%)
  Pallas kernels  207 us (41%)
  between operations  13.5 us (3%)
  starting transfers between devices  8.4 us (2%)
  local copies, waits for them, and re-layouts  7.15 us (1%)
    pallas_call x1, Pallas kernels, convolve(): pl.pallas_call(functools.partial(convolve_kernel, owners), in_specs=[pl.B...  207 us
    all_gather x1, waiting for transfers between devices, body(): lax.all_gather(response.reshape(-1, SW), 'freq', axis=0, tiled=True)  192 us
    all_gather x1, waiting for transfers between devices, body(): response = lax.all_gather(response, 'panel', axis=0, tiled=True)  51 us
    all_to_all x1, waiting for transfers between devices, body(): lax.all_to_all(shot_gathers[:, :, :SW], 'freq', split_axis=1, concat_axis...  24 us
  transfers between devices with their start and end apart: 3, of which 3 were waited for; matrix products, arithmetic and copies ran while one was open for 0% of the time, Pallas kernels for 0%

profile of v3, /device:TPU:0, one launch (start us, length us, event | category | flops | bytes accessed | tf_op | source)
XLA Modules:
  0.0 505.4 jit_solution(17129399648940402087)
XLA Ops:
  6.5 0.0 slice-start
  6.5 1.2 slice-done
  7.8 0.0 copy-start
  7.8 0.0 copy-start.1
  7.8 1.8 copy.17
  9.5 8.3 %all-to-all-start = ((bf16[4,1024,128]{2,0,1:T(4,128)(2,1)}), bf16[4,1024,128]{2,0,1:T(4,128)(2,1)S(1)}, u32[]{:S(2)}, u32[]{:S(2)}) async-start(bf16[4,1024,128]{2,0,1:T(4,128)(2,1)} %copy.17), calls=%async_computation | async-start | bytes 2097152 | tf_op jit(solution)/shard_map/all_to_all | solution.py:241
  17.9 0.0 all-gather.3.cloned.1.call-start
  17.9 0.0 copy-done
  18.0 0.0 copy-done.1
  18.0 0.2 fusion.13
  18.1 0.2 select_select_fusion
  18.3 24.0 %all-to-all-done = bf16[4,1024,128]{2,0,1:T(4,128)(2,1)S(1)} async-done(((bf16[4,1024,128]{2,0,1:T(4,128)(2,1)}), bf16[4,1024,128]{2,0,1:T(4,128)(2,1)S(1)}, u32[]{:S(2)}, u32[]{:S(2)}) %all-to-all-start) | async-done | bytes 1048608 | tf_op jit(solution)/shard_map/all_to_all | solution.py:241
  42.3 0.1 copy.9
  42.5 0.1 copy.10
  42.5 1.0 multiply_convert_fusion
  43.5 1.1 bitcast_convert_fusion
  44.6 1.6 copy.12
  46.2 0.0 all-gather.3.cloned.1.call-update
  46.3 0.0 all-gather.5.cloned.1.call-start
  46.3 191.9 %all-gather.3.cloned.1.call-done = bf16[65536,128]{1,0:T(8,128)(2,1)} async-done(((bf16[4096,128]{1,0:T(8,128)(2,1)}), bf16[65536,128]{1,0:T(8,128)(2,1)}) %all-gather.3.cloned.1.call-update) | async-done | bytes 16777232 | tf_op jit(solution)/shard_map/all_gather | solution.py:246
  238.2 0.0 all-gather.5.cloned.1.call-update
  238.3 51.0 %all-gather.5.cloned.1.call-done = bf16[131072,128]{1,0:T(8,128)(2,1)} async-done(((bf16[65536,128]{1,0:T(8,128)(2,1)}), bf16[131072,128]{1,0:T(8,128)(2,1)}) %all-gather.5.cloned.1.call-update) | async-done | bytes 33554448 | tf_op jit(solution)/shard_map/all_gather | solution.py:247
  289.2 207.0 %shard_map.37 = bf16[4,1024,128]{2,1,0:T(8,128)(2,1)} custom-call(bf16[4,1024,2048]{2,1,0:T(8,128)(2,1)} %d_hbm.1, bf16[32,64,64,128]{3,2,1,0:T(8,128)(2,1)} %bitcast.21), custom_call_target="tpu_custom_call" | custom-call | flops 137438953472 | bytes 117440512 | tf_op jit(solution)/shard_map/pallas_call | solution.py:181
  496.3 2.3 copy.21
  (3 shorter events, 0.0 us)
Async XLA Ops:
  6.5 1.2 slice-start
  7.8 10.2 %copy-start = (s32[32]{0:T(128)S(1)}, s32[32]{0:T(128)}, u32[]{:S(2)}) copy-start(s32[32]{0:T(128)} %param.5) | copy-start | bytes 388
  7.8 10.2 %copy-start.1 = (s32[32]{0:T(128)S(1)}, s32[32]{0:T(128)}, u32[]{:S(2)}) copy-start(s32[32]{0:T(128)} %param.4) | copy-start | bytes 388
  9.5 32.8 %all-to-all-start = ((bf16[4,1024,128]{2,0,1:T(4,128)(2,1)}), bf16[4,1024,128]{2,0,1:T(4,128)(2,1)S(1)}, u32[]{:S(2)}, u32[]{:S(2)}) async-start(bf16[4,1024,128]{2,0,1:T(4,128)(2,1)} %copy.17), calls=%async_computation | async-start | bytes 2097152 | tf_op jit(solution)/shard_map/all_to_all | solution.py:241
  17.9 220.4 %all-gather.3.cloned.1.call-start = ((), (), s32[]{:S(2)}) async-start(), calls=%async_computation.1 | async-start | bytes 17825792 | tf_op jit(solution)/shard_map/all_gather | solution.py:246
  46.3 243.0 %all-gather.5.cloned.1.call-start = ((), (), s32[]{:S(2)}) async-start(), calls=%async_computation.2 | async-start | bytes 50331648 | tf_op jit(solution)/shard_map/all_gather | solution.py:247
Sparse Core Ops, SparseCore 0:
  46.4 191.8 all-gather.2
  239.8 49.4 all-gather.4
